TPU v7x, 128 devices: a whole 4x4x4 slice. The times are simulated.
128 devices in a mesh: section: 8 (over y, z_hi), tensor: 16 (over x, z_lo, core).
Axes of the slice: x: 4, y: 4, z: 4 (z_hi: 2, z_lo: 2; z = z_hi * 2 + z_lo), core: 2. Of those that a mesh axis runs over, the one named last changes fastest.
Arguments:
- top_grad: bfloat16 [1, 2048, 2304], P(None, 'tensor'), may hold values from -6 to 6
- down_weight: bfloat16 [8, 18432, 2304], P('section', 'tensor'), may hold values from -0.046875 to 0.046875
- up_weight: bfloat16 [8, 2304, 18432], P('section', None, 'tensor'), may hold values from -0.125 to 0.125
- gate_pre: bfloat16 [8, 1, 2048, 18432], P('section', None, None, 'tensor'), may hold values from -6 to 6
Outputs:
- input_grad: bfloat16 [8, 1, 2048, 2304], P('section', None, 'tensor')
All inputs are finite; a program needn't handle non-finite values.
Results may differ from a plain program's by a relative error of at most 0.04.
Values may be sent and summed in bfloat16 or wider, within the bound.
A program may use at most 128 MiB of HBM per device.

v0:
```python
import jax
import jax.numpy as jnp
from jax import lax
from jax.sharding import PartitionSpec as P


def passed_along(block, axis, distance):
    devices = range(lax.axis_size(axis))
    route = [(i - distance, i) for i in devices if i - distance in devices]
    return lax.ppermute(block, axis, route)


def on_device(top_grad, down_weight, up_weight, gate_pre):
    sections = lax.axis_size("section")
    tensor_count = lax.axis_size("tensor")
    section_index = lax.axis_index("section")
    micro_count, row_count, feature_count = top_grad.shape
    hidden_cols = gate_pre.shape[-1]
    pieces = 1
    unit_rows = row_count // pieces
    unit_count = micro_count * pieces
    gate_units = gate_pre[0].reshape(micro_count, tensor_count, pieces, unit_rows, hidden_cols)
    gate_units = gate_units.transpose(0, 2, 1, 3, 4).reshape(
        unit_count, tensor_count * unit_rows, hidden_cols
    )
    down_proj = down_weight[0]
    up_proj = up_weight[0]

    def backward_unit(grad_rows, gate_rows, usable):

        def compute_hidden(operands):
            rows_in, gate_in = operands
            grad_hidden = lax.dot_general(
                rows_in, down_proj, (((1,), (1,)), ((), ())), preferred_element_type=jnp.float32
            )
            gate_value = jax.nn.gelu(gate_in.astype(jnp.float32), approximate=True)
            return (grad_hidden * gate_value).astype(jnp.bfloat16)

        def empty_hidden(operands):
            return jnp.zeros((operands[0].shape[0], hidden_cols), jnp.bfloat16)

        grad_up = lax.cond(
            usable,
            compute_hidden,
            empty_hidden,
            (lax.all_gather(grad_rows, "tensor", axis=0, tiled=True), gate_rows),
        )

        def compute_partial(block_in):
            return lax.dot_general(
                block_in, up_proj, (((1,), (1,)), ((), ())), preferred_element_type=jnp.float32
            )

        def empty_partial(block_in):
            return jnp.zeros((block_in.shape[0], feature_count), jnp.float32)

        branch = lax.psum_scatter(
            lax.cond(usable, compute_partial, empty_partial, grad_up).astype(jnp.bfloat16),
            "tensor",
            scatter_dimension=0,
            tiled=True,
        ).astype(jnp.float32)
        return (grad_rows.astype(jnp.float32) + branch).astype(jnp.bfloat16)

    def advance(tick_index, state_pair):
        incoming, results = state_pair
        unit_index = tick_index - (sections - 1 - section_index)
        usable = (unit_index >= 0) & (unit_index < unit_count)
        position = jnp.clip(unit_index, 0, unit_count - 1)
        from_top = lax.dynamic_index_in_dim(top_grad, position, 0, keepdims=False)
        grad_rows = jnp.where(section_index == sections - 1, from_top, incoming)
        gate_rows = lax.dynamic_index_in_dim(gate_units, position, 0, keepdims=False)
        computed = backward_unit(grad_rows, gate_rows, usable)
        produced = jnp.where(usable, computed, jnp.zeros_like(computed))
        previous = lax.dynamic_index_in_dim(results, position, 0, keepdims=False)
        stored = jnp.where(usable, produced, previous)
        results = lax.dynamic_update_index_in_dim(results, stored, position, 0)
        handed = passed_along(produced, "section", -1)
        return (handed, results)

    initial = (
        jnp.zeros((unit_rows, feature_count), jnp.bfloat16),
        jnp.zeros((unit_count, unit_rows, feature_count), jnp.bfloat16),
    )
    _, results = lax.fori_loop(0, sections + unit_count - 1, advance, initial)
    return results.reshape(1, micro_count, row_count, feature_count)


def solution(mesh):
    placed = (
        P(None, "tensor", None),
        P("section", "tensor", None),
        P("section", None, "tensor"),
        P("section", None, None, "tensor"),
    )
    return jax.shard_map(
        on_device,
        mesh=mesh,
        in_specs=placed,
        out_specs=P("section", None, "tensor", None),
        check_vma=False,
    )
```

profile of v0, /device:TPU:1, one launch (start us, length us, event | category | flops | bytes accessed | tf_op | source)
XLA Modules:
  0.0 1806.7 jit_solution(15133280844812620478)
XLA Ops:
  6.6 1792.8 %while.17 = (s32[]{:T(128)}, bf16[128,2304]{1,0:T(8,128)(2,1)S(1)}, bf16[1,128,2304]{2,1,0:T(8,128)(2,1)S(1)}, s32[]{:T(128)}, pred[]{:T(512)}, /*index=5*/bf16[...) while((s32[]{:T(128)}, bf16[128,2304]{1,0:T(8,128)(2,1)S(1)}, ...), condition=%wide.region_6.7_spmd, body=%wide.region_0.6_spmd.sunk | while | flops 21771288576 | bytes 113246560 | solution.py:85
  8.7 61.2 %all-gather.2.cloned.1.call-done = bf16[2048,2304]{1,0:T(8,128)(2,1)} async-done(((bf16[128,2304]{1,0:T(8,128)(2,1)}), bf16[2048,2304]{1,0:T(8,128)(2,1)}) %all-gather.2.cloned.1.call-update) | async-done | bytes 9437200 | tf_op jit(solution)/shard_map/while/body/eval_jaxpr/all_gather | solution.py:46
  72.5 4.3 conditional.5
  76.8 138.0 %reduce-scatter.2.cloned.1.call-done = bf16[128,2304]{1,0:T(8,128)(2,1)} async-done(((bf16[2048,2304]{1,0:T(8,128)(2,1)}), bf16[128,2304]{1,0:T(8,128)(2,1)}) %reduce-scatter.2.cloned.1.call-update) | async-done | bytes 589840 | tf_op jit(solution)/shard_map/while/body/eval_jaxpr/reduce_scatter | solution.py:57
  217.5 15.8 collective-permute-done
  235.3 60.2 %all-gather.2.cloned.1.call-done = bf16[2048,2304]{1,0:T(8,128)(2,1)} async-done(((bf16[128,2304]{1,0:T(8,128)(2,1)}), bf16[2048,2304]{1,0:T(8,128)(2,1)}) %all-gather.2.cloned.1.call-update) | async-done | bytes 9437200 | tf_op jit(solution)/shard_map/while/body/eval_jaxpr/all_gather | solution.py:46
  298.1 4.3 conditional.5
  302.4 136.5 %reduce-scatter.2.cloned.1.call-done = bf16[128,2304]{1,0:T(8,128)(2,1)} async-done(((bf16[2048,2304]{1,0:T(8,128)(2,1)}), bf16[128,2304]{1,0:T(8,128)(2,1)}) %reduce-scatter.2.cloned.1.call-update) | async-done | bytes 589840 | tf_op jit(solution)/shard_map/while/body/eval_jaxpr/reduce_scatter | solution.py:57
  441.6 15.8 collective-permute-done
  459.4 59.9 %all-gather.2.cloned.1.call-done = bf16[2048,2304]{1,0:T(8,128)(2,1)} async-done(((bf16[128,2304]{1,0:T(8,128)(2,1)}), bf16[2048,2304]{1,0:T(8,128)(2,1)}) %all-gather.2.cloned.1.call-update) | async-done | bytes 9437200 | tf_op jit(solution)/shard_map/while/body/eval_jaxpr/all_gather | solution.py:46
  521.8 4.3 conditional.5
  526.1 138.3 %reduce-scatter.2.cloned.1.call-done = bf16[128,2304]{1,0:T(8,128)(2,1)} async-done(((bf16[2048,2304]{1,0:T(8,128)(2,1)}), bf16[128,2304]{1,0:T(8,128)(2,1)}) %reduce-scatter.2.cloned.1.call-update) | async-done | bytes 589840 | tf_op jit(solution)/shard_map/while/body/eval_jaxpr/reduce_scatter | solution.py:57
  667.1 15.8 collective-permute-done
  684.9 60.2 %all-gather.2.cloned.1.call-done = bf16[2048,2304]{1,0:T(8,128)(2,1)} async-done(((bf16[128,2304]{1,0:T(8,128)(2,1)}), bf16[2048,2304]{1,0:T(8,128)(2,1)}) %all-gather.2.cloned.1.call-update) | async-done | bytes 9437200 | tf_op jit(solution)/shard_map/while/body/eval_jaxpr/all_gather | solution.py:46
  752.0 136.8 %reduce-scatter.2.cloned.1.call-done = bf16[128,2304]{1,0:T(8,128)(2,1)} async-done(((bf16[2048,2304]{1,0:T(8,128)(2,1)}), bf16[128,2304]{1,0:T(8,128)(2,1)}) %reduce-scatter.2.cloned.1.call-update) | async-done | bytes 589840 | tf_op jit(solution)/shard_map/while/body/eval_jaxpr/reduce_scatter | solution.py:57
  891.4 15.8 collective-permute-done
  909.2 60.2 %all-gather.2.cloned.1.call-done = bf16[2048,2304]{1,0:T(8,128)(2,1)} async-done(((bf16[128,2304]{1,0:T(8,128)(2,1)}), bf16[2048,2304]{1,0:T(8,128)(2,1)}) %all-gather.2.cloned.1.call-update) | async-done | bytes 9437200 | tf_op jit(solution)/shard_map/while/body/eval_jaxpr/all_gather | solution.py:46
  976.3 136.8 %reduce-scatter.2.cloned.1.call-done = bf16[128,2304]{1,0:T(8,128)(2,1)} async-done(((bf16[2048,2304]{1,0:T(8,128)(2,1)}), bf16[128,2304]{1,0:T(8,128)(2,1)}) %reduce-scatter.2.cloned.1.call-update) | async-done | bytes 589840 | tf_op jit(solution)/shard_map/while/body/eval_jaxpr/reduce_scatter | solution.py:57
  1115.8 15.7 collective-permute-done
  1133.5 60.2 %all-gather.2.cloned.1.call-done = bf16[2048,2304]{1,0:T(8,128)(2,1)} async-done(((bf16[128,2304]{1,0:T(8,128)(2,1)}), bf16[2048,2304]{1,0:T(8,128)(2,1)}) %all-gather.2.cloned.1.call-update) | async-done | bytes 9437200 | tf_op jit(solution)/shard_map/while/body/eval_jaxpr/all_gather | solution.py:46
  1200.6 135.3 %reduce-scatter.2.cloned.1.call-done = bf16[128,2304]{1,0:T(8,128)(2,1)} async-done(((bf16[2048,2304]{1,0:T(8,128)(2,1)}), bf16[128,2304]{1,0:T(8,128)(2,1)}) %reduce-scatter.2.cloned.1.call-update) | async-done | bytes 589840 | tf_op jit(solution)/shard_map/while/body/eval_jaxpr/reduce_scatter | solution.py:57
  1338.6 15.7 collective-permute-done
  1356.3 60.2 %all-gather.2.cloned.1.call-done = bf16[2048,2304]{1,0:T(8,128)(2,1)} async-done(((bf16[128,2304]{1,0:T(8,128)(2,1)}), bf16[2048,2304]{1,0:T(8,128)(2,1)}) %all-gather.2.cloned.1.call-update) | async-done | bytes 9437200 | tf_op jit(solution)/shard_map/while/body/eval_jaxpr/all_gather | solution.py:46
  1423.4 135.9 %reduce-scatter.2.cloned.1.call-done = bf16[128,2304]{1,0:T(8,128)(2,1)} async-done(((bf16[2048,2304]{1,0:T(8,128)(2,1)}), bf16[128,2304]{1,0:T(8,128)(2,1)}) %reduce-scatter.2.cloned.1.call-update) | async-done | bytes 589840 | tf_op jit(solution)/shard_map/while/body/eval_jaxpr/reduce_scatter | solution.py:57
  1562.0 15.7 collective-permute-done
  1579.7 59.9 %all-gather.2.cloned.1.call-done = bf16[2048,2304]{1,0:T(8,128)(2,1)} async-done(((bf16[128,2304]{1,0:T(8,128)(2,1)}), bf16[2048,2304]{1,0:T(8,128)(2,1)}) %all-gather.2.cloned.1.call-update) | async-done | bytes 9437200 | tf_op jit(solution)/shard_map/while/body/eval_jaxpr/all_gather | solution.py:46
  1639.6 19.8 %conditional.4 = (bf16[2048,1152]{1,0:T(8,128)(2,1)}) conditional(s32[]{:T(128)} %convert_element_type.70, () %tuple.55, (bf16[2048,2304]{1,0:T(8,128)(2,1)}, bf16[1152,2304]{1,0:T(8,128)(2,1)}, bf16[1,2048,1152]{2,1,0:T(8,128)(2,1)}) %tuple.56), branch_computations={%region_1.1_spmd, %region_2.2_spmd} | conditional | flops 10897588224 | bytes 24182792 | solution.py:42
  1639.6 19.8 %fusion.5 = bf16[2048,1152]{1,0:T(8,128)(2,1)} fusion(bf16[2048,2304]{1,0:T(8,128)(2,1)} %get-tuple-element.219, bf16[1152,2304]{1,0:T(8,128)(2,1)} %get-tuple-element.220, bf16[1,2048,1152]{2,1,0:T(8,128)(2,1)} %get-tuple-element.221), kind=kOutput, calls=%fused_computation.10 | convolution fusion | flops 10897588224 | bytes 24182784 | tf_op jit(solution)/shard_map/while/body/eval_jaxpr/cond/branch_1_fun/dot_general | solution.py:33
  1659.4 18.0 conditional.5
  1659.4 18.0 fusion.9
  1677.4 103.4 %reduce-scatter.2.cloned.1.call-done = bf16[128,2304]{1,0:T(8,128)(2,1)} async-done(((bf16[2048,2304]{1,0:T(8,128)(2,1)}), bf16[128,2304]{1,0:T(8,128)(2,1)}) %reduce-scatter.2.cloned.1.call-update) | async-done | bytes 589840 | tf_op jit(solution)/shard_map/while/body/eval_jaxpr/reduce_scatter | solution.py:57
  1783.5 15.9 collective-permute-done
  (101 shorter events, 121.3 us)
Async XLA Ops:
  6.6 63.3 %all-gather.2.cloned.1.call-start = ((), (), s32[]{:S(2)}) async-start(), calls=%async_computation.1 | async-start | bytes 10027008 | tf_op jit(solution)/shard_map/while/body/eval_jaxpr/all_gather | solution.py:46
  8.7 206.2 %reduce-scatter.2.cloned.1.call-start = ((), (), s32[]{:S(2)}) async-start(), calls=%async_computation.2 | async-start | bytes 10027008 | tf_op jit(solution)/shard_map/while/body/eval_jaxpr/reduce_scatter | solution.py:57
  76.8 138.1 %copy-start = (bf16[128,2304]{1,0:T(8,128)(2,1)S(1)}, bf16[128,2304]{1,0:T(8,128)(2,1)}, u32[]{:S(2)}) copy-start(bf16[128,2304]{1,0:T(8,128)(2,1)} %bitcast_select_fusion.3) | copy-start | bytes 1769476 | tf_op jit(solution)/shard_map/while
  216.2 17.1 collective-permute-start
  233.3 62.2 %all-gather.2.cloned.1.call-start = ((), (), s32[]{:S(2)}) async-start(), calls=%async_computation.1 | async-start | bytes 10027008 | tf_op jit(solution)/shard_map/while/body/eval_jaxpr/all_gather | solution.py:46
  235.3 203.6 %reduce-scatter.2.cloned.1.call-start = ((), (), s32[]{:S(2)}) async-start(), calls=%async_computation.2 | async-start | bytes 10027008 | tf_op jit(solution)/shard_map/while/body/eval_jaxpr/reduce_scatter | solution.py:57
  302.3 136.6 %copy-start = (bf16[128,2304]{1,0:T(8,128)(2,1)S(1)}, bf16[128,2304]{1,0:T(8,128)(2,1)}, u32[]{:S(2)}) copy-start(bf16[128,2304]{1,0:T(8,128)(2,1)} %bitcast_select_fusion.3) | copy-start | bytes 1769476 | tf_op jit(solution)/shard_map/while
  440.3 17.1 collective-permute-start
  457.4 61.9 %all-gather.2.cloned.1.call-start = ((), (), s32[]{:S(2)}) async-start(), calls=%async_computation.1 | async-start | bytes 10027008 | tf_op jit(solution)/shard_map/while/body/eval_jaxpr/all_gather | solution.py:46
  459.3 205.1 %reduce-scatter.2.cloned.1.call-start = ((), (), s32[]{:S(2)}) async-start(), calls=%async_computation.2 | async-start | bytes 10027008 | tf_op jit(solution)/shard_map/while/body/eval_jaxpr/reduce_scatter | solution.py:57
  526.1 138.4 %copy-start = (bf16[128,2304]{1,0:T(8,128)(2,1)S(1)}, bf16[128,2304]{1,0:T(8,128)(2,1)}, u32[]{:S(2)}) copy-start(bf16[128,2304]{1,0:T(8,128)(2,1)} %bitcast_select_fusion.3) | copy-start | bytes 1769476 | tf_op jit(solution)/shard_map/while
  665.8 17.1 collective-permute-start
  682.9 62.2 %all-gather.2.cloned.1.call-start = ((), (), s32[]{:S(2)}) async-start(), calls=%async_computation.1 | async-start | bytes 10027008 | tf_op jit(solution)/shard_map/while/body/eval_jaxpr/all_gather | solution.py:46
  684.9 203.9 %reduce-scatter.2.cloned.1.call-start = ((), (), s32[]{:S(2)}) async-start(), calls=%async_computation.2 | async-start | bytes 10027008 | tf_op jit(solution)/shard_map/while/body/eval_jaxpr/reduce_scatter | solution.py:57
  751.9 136.8 %copy-start = (bf16[128,2304]{1,0:T(8,128)(2,1)S(1)}, bf16[128,2304]{1,0:T(8,128)(2,1)}, u32[]{:S(2)}) copy-start(bf16[128,2304]{1,0:T(8,128)(2,1)} %bitcast_select_fusion.3) | copy-start | bytes 1769476 | tf_op jit(solution)/shard_map/while
  890.1 17.1 collective-permute-start
  907.2 62.2 %all-gather.2.cloned.1.call-start = ((), (), s32[]{:S(2)}) async-start(), calls=%async_computation.1 | async-start | bytes 10027008 | tf_op jit(solution)/shard_map/while/body/eval_jaxpr/all_gather | solution.py:46
  909.2 203.9 %reduce-scatter.2.cloned.1.call-start = ((), (), s32[]{:S(2)}) async-start(), calls=%async_computation.2 | async-start | bytes 10027008 | tf_op jit(solution)/shard_map/while/body/eval_jaxpr/reduce_scatter | solution.py:57
  976.3 136.8 %copy-start = (bf16[128,2304]{1,0:T(8,128)(2,1)S(1)}, bf16[128,2304]{1,0:T(8,128)(2,1)}, u32[]{:S(2)}) copy-start(bf16[128,2304]{1,0:T(8,128)(2,1)} %bitcast_select_fusion.3) | copy-start | bytes 1769476 | tf_op jit(solution)/shard_map/while
  1114.5 17.0 collective-permute-start
  1131.5 62.2 %all-gather.2.cloned.1.call-start = ((), (), s32[]{:S(2)}) async-start(), calls=%async_computation.1 | async-start | bytes 10027008 | tf_op jit(solution)/shard_map/while/body/eval_jaxpr/all_gather | solution.py:46
  1133.5 202.4 %reduce-scatter.2.cloned.1.call-start = ((), (), s32[]{:S(2)}) async-start(), calls=%async_computation.2 | async-start | bytes 10027008 | tf_op jit(solution)/shard_map/while/body/eval_jaxpr/reduce_scatter | solution.py:57
  1200.6 135.3 %copy-start = (bf16[128,2304]{1,0:T(8,128)(2,1)S(1)}, bf16[128,2304]{1,0:T(8,128)(2,1)}, u32[]{:S(2)}) copy-start(bf16[128,2304]{1,0:T(8,128)(2,1)} %bitcast_select_fusion.3) | copy-start | bytes 1769476 | tf_op jit(solution)/shard_map/while
  1337.3 17.0 collective-permute-start
  1354.3 62.2 %all-gather.2.cloned.1.call-start = ((), (), s32[]{:S(2)}) async-start(), calls=%async_computation.1 | async-start | bytes 10027008 | tf_op jit(solution)/shard_map/while/body/eval_jaxpr/all_gather | solution.py:46
  1356.3 203.0 %reduce-scatter.2.cloned.1.call-start = ((), (), s32[]{:S(2)}) async-start(), calls=%async_computation.2 | async-start | bytes 10027008 | tf_op jit(solution)/shard_map/while/body/eval_jaxpr/reduce_scatter | solution.py:57
  1423.4 135.9 %copy-start = (bf16[128,2304]{1,0:T(8,128)(2,1)S(1)}, bf16[128,2304]{1,0:T(8,128)(2,1)}, u32[]{:S(2)}) copy-start(bf16[128,2304]{1,0:T(8,128)(2,1)} %bitcast_select_fusion.3) | copy-start | bytes 1769476 | tf_op jit(solution)/shard_map/while
  1560.7 17.0 collective-permute-start
  1577.7 61.9 %all-gather.2.cloned.1.call-start = ((), (), s32[]{:S(2)}) async-start(), calls=%async_computation.1 | async-start | bytes 10027008 | tf_op jit(solution)/shard_map/while/body/eval_jaxpr/all_gather | solution.py:46
  1579.7 201.2 %reduce-scatter.2.cloned.1.call-start = ((), (), s32[]{:S(2)}) async-start(), calls=%async_computation.2 | async-start | bytes 10027008 | tf_op jit(solution)/shard_map/while/body/eval_jaxpr/reduce_scatter | solution.py:57
  1677.4 103.5 %copy-start = (bf16[128,2304]{1,0:T(8,128)(2,1)S(1)}, bf16[128,2304]{1,0:T(8,128)(2,1)}, u32[]{:S(2)}) copy-start(bf16[128,2304]{1,0:T(8,128)(2,1)} %bitcast_select_fusion.3) | copy-start | bytes 1769476 | tf_op jit(solution)/shard_map/while
  1782.2 17.2 collective-permute-start
  (1 other events, 0.8 us)
Sparse Core Ops, SparseCore 0:
  9.2 60.7 all-gather.1
  76.9 137.8 reduce-scatter.1
  235.8 59.6 all-gather.1
  302.5 136.3 reduce-scatter.1
  459.6 59.6 all-gather.1
  526.2 138.1 reduce-scatter.1
  685.4 59.6 all-gather.1
  752.1 136.6 reduce-scatter.1
  909.7 59.6 all-gather.1
  976.4 136.6 reduce-scatter.1
  1134.0 59.6 all-gather.1
  1200.7 135.1 reduce-scatter.1
  1356.9 59.6 all-gather.1
  1423.5 135.7 reduce-scatter.1
  1579.9 59.6 all-gather.1
  1677.5 103.2 reduce-scatter.1
where the time goes:
time: 1810 us
  waiting for transfers between devices  1670 us (92%)
  local copies, waits for them, and re-layouts  48.7 us (3%)
  matrix products  37.7 us (2%)
  other arithmetic  26.5 us (1%)
    reduce_scatter x8, waiting for transfers between devices, backward_unit(): lax.psum_scatter(lax.cond(usable, compute_partial, empty_partial, grad_up...  1060 us
    all_gather x8, waiting for transfers between devices, backward_unit(): lax.all_gather(grad_rows, 'tensor', axis=0, tiled=True)  482 us
    ppermute x8, waiting for transfers between devices, passed_along(): return lax.ppermute(block, axis, route)  126 us
    another operation x15, local copies, waits for them, and re-layouts  47.8 us
  transfers between devices with their start and end apart: 24, of which 24 were waited for; matrix products, arithmetic and copies ran while one was open for 0% of the time, Pallas kernels for 0%

commit v1 on v0

v1 whole, which is shorter than its diff:
```python
import functools

import jax
import jax.numpy as jnp
from jax import lax
from jax.experimental import pallas as pl
from jax.experimental.pallas import tpu as pltpu
from jax.sharding import PartitionSpec as P

MESH = pl.DeviceIdType.MESH
BLOCK = 16
F32 = jnp.float32
BF16 = jnp.bfloat16
NN = (((1,), (0,)), ((), ()))


def gelu(v):
    return 0.5 * v * (1.0 + jnp.tanh(0.7978845608028654 * (v + 0.044715 * (v * v * v))))


def kernel(
    sections, chips, chunks,
    top_hbm, down_hbm, up_hbm, gate_hbm, out_hbm,
    top, down, up, gate, feed, held, act, hidden, grad_up, own_part, sib_part, sib_recv, pair, terms, result, out,
    load_sem, feed_send, feed_recv, own_sem, in_send, in_recv, swap_send, swap_recv, part_send, part_recv,
    term_send, term_recv, out_send, out_recv, store_sem,
):
    section = lax.axis_index("section")
    tensor = lax.axis_index("tensor")
    chip = lax.div(tensor, 2)
    core = lax.rem(tensor, 2)
    other = 1 - core
    sibling = chip * 2 + other
    half = held.shape[-1]
    per_core = chunks // 2
    last = sections - 1

    def wait_for(ref, sem):
        pltpu.make_async_copy(ref, ref, sem).wait()

    def remote(src, dst, send, recv, to_section, to_tensor):
        return pltpu.make_async_remote_copy(
            src_ref=src, dst_ref=dst, send_sem=send, recv_sem=recv,
            device_id={"section": to_section, "tensor": to_tensor}, device_id_type=MESH,
        )

    def rows_of(index):
        return pl.ds(pl.multiple_of(index * BLOCK, BLOCK), BLOCK)

    def cols_of(index):
        return pl.ds(pl.multiple_of(index * half, 128), half)

    loads = [
        pltpu.make_async_copy(top_hbm, top, load_sem.at[0]),
        pltpu.make_async_copy(gate_hbm, gate, load_sem.at[1]),
        pltpu.make_async_copy(down_hbm, down, load_sem.at[2]),
        pltpu.make_async_copy(up_hbm, up, load_sem.at[3]),
    ]
    for load in loads:
        load.start()

    barrier = pltpu.get_barrier_semaphore()

    def greet(to_section, to_tensor):
        pl.semaphore_signal(
            barrier, inc=1, device_id={"section": to_section, "tensor": to_tensor}, device_id_type=MESH
        )

    greet(section, sibling)
    for step in range(1, chips):
        greet(section, lax.rem(chip + step, chips) * 2 + core)

    @pl.when(section > 0)
    def _():
        for step in range(chips):
            greet(section - 1, lax.rem(chip + step, chips) * 2 + core)

    @pl.when(section < last)
    def _():
        for step in range(chips):
            greet(section + 1, lax.rem(chip + step, chips) * 2 + core)

    pl.semaphore_wait(
        barrier, chips + jnp.where(section > 0, chips, 0) + jnp.where(section < last, chips, 0)
    )

    loads[0].wait()

    def send_feed(c):
        block = feed.at[pl.ds(pl.multiple_of(c * BLOCK, BLOCK), BLOCK)]
        for step in range(1, chips):
            remote(
                block, held.at[c, core, rows_of(chip)], in_send.at[c], in_recv.at[c],
                section, lax.rem(chip + step, chips) * 2 + core,
            ).start()
        pltpu.make_async_copy(block, held.at[c, core, rows_of(chip)], in_recv.at[c]).start()

    rows_here = per_core * BLOCK

    @pl.when(section == last)
    def _():
        mine = feed.at[pl.ds(pl.multiple_of(core * rows_here, BLOCK), rows_here)]
        swap = remote(top.at[:, cols_of(other)], mine, feed_send, feed_recv, section, sibling)
        swap.start()
        keep = pltpu.make_async_copy(top.at[:, cols_of(core)], mine, own_sem)
        keep.start()
        keep.wait()
        swap.wait()
        send_feed(0)
        if chunks > 1:
            send_feed(1)

    loads[1].wait()

    def finish(c):
        wait_for(terms.at[c, pl.ds(0, chips - 1)], term_recv.at[c])
        total = held[c, core, rows_of(chip), :].astype(F32)
        for j in range(chips):
            total = total + terms[c, j].astype(F32)
        result[c] = total.astype(BF16)

        @pl.when(section > 0)
        def _():
            for step in range(chips):
                remote(
                    result.at[c], held.at[c, core, rows_of(chip)], in_send.at[c], in_recv.at[c],
                    section - 1, lax.rem(chip + step, chips) * 2 + core,
                ).start()

        place = lax.rem(c, per_core)

        @pl.when(lax.div(c, per_core) == core)
        def _():
            out[core, rows_of(place), :] = result[c]

        @pl.when(lax.div(c, per_core) == other)
        def _():
            remote(
                result.at[c], out.at[core, rows_of(place)], out_send, out_recv, section, sibling
            ).start()

    def chunk_step(c, carry):
        act[...] = gelu(gate[:, c].reshape(chips * BLOCK, -1).astype(F32))

        wait_for(held.at[c, core], in_recv.at[c])
        remote(
            held.at[c, core], held.at[c, core], swap_send.at[c], swap_recv.at[c], section, sibling
        ).start()

        @pl.when(c == 0)
        def _():
            loads[2].wait()

        hidden[...] = lax.dot_general(held[c, core], down[core], NN, preferred_element_type=F32)
        wait_for(held.at[c, other], swap_recv.at[c])
        total = hidden[...] + lax.dot_general(
            held[c, other], down[other], NN, preferred_element_type=F32
        )
        grad_up[...] = (total * act[...]).astype(BF16)

        @pl.when(c == 0)
        def _():
            loads[3].wait()

        sib_part[c] = lax.dot_general(
            grad_up[...], up[other], NN, preferred_element_type=F32
        ).astype(BF16)
        remote(
            sib_part.at[c], sib_recv.at[c], part_send.at[c], part_recv.at[c], section, sibling
        ).start()
        own_part[...] = lax.dot_general(grad_up[...], up[core], NN, preferred_element_type=F32)

        @pl.when(c > 0)
        def _():
            finish(c - 1)

        wait_for(sib_recv.at[c], part_recv.at[c])
        pair[c] = (own_part[...] + sib_recv[c].astype(F32)).astype(BF16)
        for step in range(1, chips):
            to_chip = lax.rem(chip + step, chips)
            remote(
                pair.at[c, rows_of(to_chip)], terms.at[c, chip], term_send.at[c], term_recv.at[c],
                section, to_chip * 2 + core,
            ).start()
        terms[c, chip] = pair[c, rows_of(chip), :]

        @pl.when((section == last) & (c + 2 < chunks))
        def _():
            send_feed(c + 2)

        return carry

    lax.fori_loop(0, chunks, chunk_step, 0)
    finish(chunks - 1)

    wait_for(out.at[other], out_recv)
    stores = [
        pltpu.make_async_copy(out.at[h], out_hbm.at[:, pl.ds(h * half, half)], store_sem.at[h])
        for h in range(2)
    ]
    for store in stores:
        store.start()

    def drain(c, carry):
        wait_for(held.at[c, core], swap_send.at[c])
        wait_for(sib_part.at[c], part_send.at[c])
        wait_for(terms.at[c, pl.ds(0, chips - 1)], term_send.at[c])

        @pl.when(section > 0)
        def _():
            wait_for(terms.at[c], in_send.at[c])

        @pl.when(section == last)
        def _():
            wait_for(terms.at[c, pl.ds(0, chips - 1)], in_send.at[c])

        return carry

    lax.fori_loop(0, chunks, drain, 0)
    wait_for(out.at[core], out_send)
    for store in stores:
        store.wait()


def on_device(sections, top_grad, down_weight, up_weight, gate_pre):
    row_count, features = top_grad.shape[-2:]
    units = gate_pre.shape[-1]
    tokens = gate_pre.shape[2]
    devices = lax.axis_size("tensor")
    chips = devices // 2
    chunks = 2 * row_count // BLOCK
    half = features // 2
    rows = chips * BLOCK
    down = down_weight[0].T.reshape(2, half, units)
    up = up_weight[0].reshape(2, half, units).transpose(0, 2, 1)
    gate = gate_pre.reshape(chips, chunks, BLOCK, units)
    dma = pltpu.SemaphoreType.DMA
    produced = pl.pallas_call(
        functools.partial(kernel, sections, chips, chunks),
        name="chain",
        out_shape=jax.ShapeDtypeStruct((row_count, features), BF16),
        in_specs=[pl.BlockSpec(memory_space=pl.ANY)] * 4,
        out_specs=pl.BlockSpec(memory_space=pl.ANY),
        scratch_shapes=[
            pltpu.VMEM((row_count, features), BF16),
            pltpu.VMEM((2, half, units), BF16),
            pltpu.VMEM((2, units, half), BF16),
            pltpu.VMEM((chips, chunks, BLOCK, units), BF16),
            pltpu.VMEM((2 * row_count, half), BF16),
            pltpu.VMEM((chunks, 2, rows, half), BF16),
            pltpu.VMEM((rows, units), F32),
            pltpu.VMEM((rows, units), F32),
            pltpu.VMEM((rows, units), BF16),
            pltpu.VMEM((rows, half), F32),
            pltpu.VMEM((chunks, rows, half), BF16),
            pltpu.VMEM((chunks, rows, half), BF16),
            pltpu.VMEM((chunks, rows, half), BF16),
            pltpu.VMEM((chunks, chips, BLOCK, half), BF16),
            pltpu.VMEM((chunks, BLOCK, half), BF16),
            pltpu.VMEM((2, row_count, half), BF16),
            dma((4,)),
            dma,
            dma,
            dma,
            dma((chunks,)),
            dma((chunks,)),
            dma((chunks,)),
            dma((chunks,)),
            dma((chunks,)),
            dma((chunks,)),
            dma((chunks,)),
            dma((chunks,)),
            dma,
            dma,
            dma((2,)),
        ],
        compiler_params=pltpu.CompilerParams(
            collective_id=0, has_side_effects=True, vmem_limit_bytes=60 * 1024 * 1024
        ),
    )(top_grad[0], down, up, gate)
    return produced[None, None]


def solution(mesh):
    placed = (
        P(None, "tensor", None),
        P("section", "tensor", None),
        P("section", None, "tensor"),
        P("section", None, None, "tensor"),
    )
    return jax.shard_map(
        functools.partial(on_device, mesh.shape["section"]),
        mesh=mesh,
        in_specs=placed,
        out_specs=P("section", None, "tensor", None),
        check_vma=False,
    )
```

time: 1810 us -> 341 us (0.19)
  waiting for transfers between devices: 1670 us -> 0 us
  Pallas kernels: 0 us -> 322 us
  matrix products: 37.7 us -> 0 us
  local copies, waits for them, and re-layouts: 48.7 us -> 19 us
  other arithmetic: 26.5 us -> 0 us
    reduce_scatter x8 -> x0, waiting for transfers between devices: 1060 us -> none  [backward_unit(): lax.psum_scatter(lax.cond(usable, compute_partial, empty_partial, grad_up...]
    all_gather x8 -> x0, waiting for transfers between devices: 482 us -> none  [backward_unit(): lax.all_gather(grad_rows, 'tensor', axis=0, tiled=True)]
    pallas_call x0 -> x1, Pallas kernels: none -> 322 us  [on_device(): pl.pallas_call(functools.partial(kernel, sections, chips, chunks), name='...]
    ppermute x8 -> x0, waiting for transfers between devices: 126 us -> none  [passed_along(): return lax.ppermute(block, axis, route)]
    another operation x15 -> x1, local copies, waits for them, and re-layouts: 47.8 us -> 8.54 us  [on_device(): up = up_weight[0].reshape(2, half, units).transpose(0, 2, 1)]
    dot_general x2 -> x0, matrix products: 37.7 us -> none  [the longest x1 19.8 us: compute_hidden(): lax.dot_general(rows_in, down_proj, (((1,), (1,)), ((), ())), preferred_e...]
  transfers between devices with their start and end apart: 24 -> 0, of which waited for: 24 -> 0; matrix products, arithmetic and copies ran while one was open for 0% -> 0% of each run, Pallas kernels for 0% -> 0%
where the time goes in v1:
time: 341 us
  Pallas kernels  322 us (94%)
  local copies, waits for them, and re-layouts  19 us (6%)
    pallas_call x1, Pallas kernels, on_device(): pl.pallas_call(functools.partial(kernel, sections, chips, chunks), name='...  322 us
    transpose x1, local copies, waits for them, and re-layouts, on_device(): down = down_weight[0].T.reshape(2, half, units)  8.56 us
    another operation x1, local copies, waits for them, and re-layouts, on_device(): up = up_weight[0].reshape(2, half, units).transpose(0, 2, 1)  8.54 us

profile of v1, /device:TPU:1, one launch (start us, length us, event | category | flops | bytes accessed | tf_op | source)
XLA Modules:
  0.0 340.8 jit_solution(11971811247127433420)
XLA Ops:
  0.0 8.6 %copy.6 = bf16[2304,1152]{1,0:T(8,128)(2,1)} copy(bf16[2304,1152]{0,1:T(8,128)(2,1)} %bitcast.11) | data formatting | bytes 10616832 | tf_op jit(solution)/shard_map/transpose | solution.py:234
  8.6 8.5 %copy.7 = bf16[2,1152,1152]{1,2,0:T(8,128)(2,1)} copy(bf16[2,1152,1152]{2,1,0:T(8,128)(2,1)} %bitcast.12) | data formatting | bytes 10616832 | tf_op jit(solution)/shard_map/reshape;squeeze | solution.py:235
  17.1 321.8 %chain.1 = bf16[128,2304]{1,0:T(8,128)(2,1)} custom-call(bf16[128,2304]{1,0:T(8,128)(2,1)} %bitcast.15, bf16[2,1152,1152]{2,1,0:T(8,128)(2,1)} %bitcast.9, bf16[2,1152,1152]{2,1,0:T(8,128)(2,1)} %bitcast.10, bf16[8,16,16,1152]{3,2,1,0:T(8,128)(2,1)} %bitcast.13), custom_call_target="tpu_custom_call" | custom-call | tf_op jit(solution)/shard_map/chain/pallas_call | solution.py:238
  338.9 1.9 copy.9

commit v2 on v1

--- a/solution.py
+++ b/solution.py
@@ -9,6 +9,7 @@
 
 MESH = pl.DeviceIdType.MESH
 BLOCK = 16
+AHEAD = 3
 F32 = jnp.float32
 BF16 = jnp.bfloat16
 NN = (((1,), (0,)), ((), ()))
@@ -21,8 +22,8 @@
 def kernel(
     sections, chips, chunks,
     top_hbm, down_hbm, up_hbm, gate_hbm, out_hbm,
-    top, down, up, gate, feed, held, act, hidden, grad_up, own_part, sib_part, sib_recv, pair, terms, result, out,
-    load_sem, feed_send, feed_recv, own_sem, in_send, in_recv, swap_send, swap_recv, part_send, part_recv,
+    top, down_raw, up_raw, down, up, gate, feed, held, act, hidden, grad_up, own_part, sib_part, sib_recv, pair, terms, result, out,
+    load_sem, feed_send, feed_recv, own_sem, hop_send, hop_recv, in_send, in_recv, swap_send, swap_recv, part_send, part_recv,
     term_send, term_recv, out_send, out_recv, store_sem,
 ):
     section = lax.axis_index("section")
@@ -53,8 +54,8 @@
     loads = [
         pltpu.make_async_copy(top_hbm, top, load_sem.at[0]),
         pltpu.make_async_copy(gate_hbm, gate, load_sem.at[1]),
-        pltpu.make_async_copy(down_hbm, down, load_sem.at[2]),
-        pltpu.make_async_copy(up_hbm, up, load_sem.at[3]),
+        pltpu.make_async_copy(down_hbm, down_raw, load_sem.at[2]),
+        pltpu.make_async_copy(up_hbm, up_raw, load_sem.at[3]),
     ]
     for load in loads:
         load.start()
@@ -70,30 +71,36 @@
     for step in range(1, chips):
         greet(section, lax.rem(chip + step, chips) * 2 + core)
 
+    facing = chip + 1 - 2 * lax.rem(chip, 2)
+
     @pl.when(section > 0)
     def _():
-        for step in range(chips):
-            greet(section - 1, lax.rem(chip + step, chips) * 2 + core)
+        greet(section - 1, facing * 2 + core)
 
     @pl.when(section < last)
     def _():
-        for step in range(chips):
-            greet(section + 1, lax.rem(chip + step, chips) * 2 + core)
-
-    pl.semaphore_wait(
-        barrier, chips + jnp.where(section > 0, chips, 0) + jnp.where(section < last, chips, 0)
-    )
+        greet(section + 1, facing * 2 + core)
+
+    pl.semaphore_wait(barrier, chips + jnp.where(section > 0, 1, 0) + jnp.where(section < last, 1, 0))
 
     loads[0].wait()
+
+    def spread(block, c, index):
+        for step in range(1, chips):
+            remote(
+                block, held.at[c, core, rows_of(index)], in_send.at[c], in_recv.at[c],
+                section, lax.rem(chip + step, chips) * 2 + core,
+            ).start()
 
     def send_feed(c):
         block = feed.at[pl.ds(pl.multiple_of(c * BLOCK, BLOCK), BLOCK)]
-        for step in range(1, chips):
-            remote(
-                block, held.at[c, core, rows_of(chip)], in_send.at[c], in_recv.at[c],
-                section, lax.rem(chip + step, chips) * 2 + core,
-            ).start()
-        pltpu.make_async_copy(block, held.at[c, core, rows_of(chip)], in_recv.at[c]).start()
+        spread(block, c, chip)
+        pltpu.make_async_copy(block, held.at[c, core, rows_of(chip)], hop_recv.at[c]).start()
+
+    def forward(c):
+        block = held.at[c, core, rows_of(facing)]
+        wait_for(block, hop_recv.at[c])
+        spread(block, c, facing)
 
     rows_here = per_core * BLOCK
 
@@ -106,9 +113,8 @@
         keep.start()
         keep.wait()
         swap.wait()
-        send_feed(0)
-        if chunks > 1:
-            send_feed(1)
+        for c in range(min(AHEAD, chunks)):
+            send_feed(c)
 
     loads[1].wait()
 
@@ -121,11 +127,10 @@
 
         @pl.when(section > 0)
         def _():
-            for step in range(chips):
-                remote(
-                    result.at[c], held.at[c, core, rows_of(chip)], in_send.at[c], in_recv.at[c],
-                    section - 1, lax.rem(chip + step, chips) * 2 + core,
-                ).start()
+            remote(
+                result.at[c], held.at[c, core, rows_of(chip)], hop_send.at[c], hop_recv.at[c],
+                section - 1, facing * 2 + core,
+            ).start()
 
         place = lax.rem(c, per_core)
 
@@ -142,25 +147,26 @@
     def chunk_step(c, carry):
         act[...] = gelu(gate[:, c].reshape(chips * BLOCK, -1).astype(F32))
 
-        wait_for(held.at[c, core], in_recv.at[c])
+        @pl.when(section == last)
+        def _():
+            wait_for(held.at[c, core, rows_of(chip)], hop_recv.at[c])
+
+        wait_for(terms.at[c, pl.ds(0, chips - 1)], in_recv.at[c])
         remote(
             held.at[c, core], held.at[c, core], swap_send.at[c], swap_recv.at[c], section, sibling
         ).start()
 
-        @pl.when(c == 0)
-        def _():
-            loads[2].wait()
-
         hidden[...] = lax.dot_general(held[c, core], down[core], NN, preferred_element_type=F32)
+
+        @pl.when((section < last) & (c + 1 < chunks))
+        def _():
+            forward(c + 1)
+
         wait_for(held.at[c, other], swap_recv.at[c])
         total = hidden[...] + lax.dot_general(
             held[c, other], down[other], NN, preferred_element_type=F32
         )
         grad_up[...] = (total * act[...]).astype(BF16)
-
-        @pl.when(c == 0)
-        def _():
-            loads[3].wait()
 
         sib_part[c] = lax.dot_general(
             grad_up[...], up[other], NN, preferred_element_type=F32
@@ -169,10 +175,6 @@
             sib_part.at[c], sib_recv.at[c], part_send.at[c], part_recv.at[c], section, sibling
         ).start()
         own_part[...] = lax.dot_general(grad_up[...], up[core], NN, preferred_element_type=F32)
-
-        @pl.when(c > 0)
-        def _():
-            finish(c - 1)
 
         wait_for(sib_recv.at[c], part_recv.at[c])
         pair[c] = (own_part[...] + sib_recv[c].astype(F32)).astype(BF16)
@@ -184,11 +186,40 @@
             ).start()
         terms[c, chip] = pair[c, rows_of(chip), :]
 
-        @pl.when((section == last) & (c + 2 < chunks))
-        def _():
-            send_feed(c + 2)
+        @pl.when((section == last) & (c + AHEAD < chunks))
+        def _():
+            send_feed(c + AHEAD)
+
+        @pl.when(c > 0)
+        def _():
+            finish(c - 1)
 
         return carry
+
+    tiles = half // 128
+
+    def turn_down(i, carry):
+        for h in range(2):
+            down[h, pl.ds(pl.multiple_of(i * 128, 128), 128), :] = down_raw[
+                :, pl.ds(pl.multiple_of(h * half + i * 128, 128), 128)
+            ].T
+        return carry
+
+    def turn_up(i, carry):
+        for h in range(2):
+            up[h, :, pl.ds(pl.multiple_of(i * 128, 128), 128)] = up_raw[
+                pl.ds(pl.multiple_of(h * half + i * 128, 128), 128), :
+            ].T
+        return carry
+
+    loads[2].wait()
+    lax.fori_loop(0, tiles, turn_down, 0)
+    loads[3].wait()
+    lax.fori_loop(0, tiles, turn_up, 0)
+
+    @pl.when(section < last)
+    def _():
+        forward(0)
 
     lax.fori_loop(0, chunks, chunk_step, 0)
     finish(chunks - 1)
@@ -206,13 +237,11 @@
         wait_for(sib_part.at[c], part_send.at[c])
         wait_for(terms.at[c, pl.ds(0, chips - 1)], term_send.at[c])
 
+        wait_for(terms.at[c, pl.ds(0, chips - 1)], in_send.at[c])
+
         @pl.when(section > 0)
         def _():
-            wait_for(terms.at[c], in_send.at[c])
-
-        @pl.when(section == last)
-        def _():
-            wait_for(terms.at[c, pl.ds(0, chips - 1)], in_send.at[c])
+            wait_for(result.at[c], hop_send.at[c])
 
         return carry
 
@@ -231,8 +260,6 @@
     chunks = 2 * row_count // BLOCK
     half = features // 2
     rows = chips * BLOCK
-    down = down_weight[0].T.reshape(2, half, units)
-    up = up_weight[0].reshape(2, half, units).transpose(0, 2, 1)
     gate = gate_pre.reshape(chips, chunks, BLOCK, units)
     dma = pltpu.SemaphoreType.DMA
     produced = pl.pallas_call(
@@ -243,6 +270,8 @@
         out_specs=pl.BlockSpec(memory_space=pl.ANY),
         scratch_shapes=[
             pltpu.VMEM((row_count, features), BF16),
+            pltpu.VMEM((units, features), BF16),
+            pltpu.VMEM((features, units), BF16),
             pltpu.VMEM((2, half, units), BF16),
             pltpu.VMEM((2, units, half), BF16),
             pltpu.VMEM((chips, chunks, BLOCK, units), BF16),
@@ -270,6 +299,8 @@
             dma((chunks,)),
             dma((chunks,)),
             dma((chunks,)),
+            dma((chunks,)),
+            dma((chunks,)),
             dma,
             dma,
             dma((2,)),
@@ -277,7 +308,7 @@
         compiler_params=pltpu.CompilerParams(
             collective_id=0, has_side_effects=True, vmem_limit_bytes=60 * 1024 * 1024
         ),
-    )(top_grad[0], down, up, gate)
+    )(top_grad[0], down_weight[0], up_weight[0], gate)
     return produced[None, None]
 
 

time: 341 us -> 268 us (0.79)
  Pallas kernels: 322 us -> 266 us
  local copies, waits for them, and re-layouts: 19 us -> 1.92 us
    pallas_call x1, Pallas kernels: 322 us -> 266 us  [on_device(): pl.pallas_call(functools.partial(kernel, sections, chips, chunks), name='...]
    transpose x1 -> x0, local copies, waits for them, and re-layouts: 8.56 us -> none  [on_device(): down = down_weight[0].T.reshape(2, half, units)]
    another operation x1 -> x0, local copies, waits for them, and re-layouts: 8.54 us -> none  [on_device(): up = up_weight[0].reshape(2, half, units).transpose(0, 2, 1)]
where the time goes in v2:
time: 268 us
  Pallas kernels  266 us (99%)
    pallas_call x1, Pallas kernels, on_device(): pl.pallas_call(functools.partial(kernel, sections, chips, chunks), name='...  266 us

profile of v2, /device:TPU:1, one launch (start us, length us, event | category | flops | bytes accessed | tf_op | source)
XLA Modules:
  0.0 267.6 jit_solution(13248763182029118787)
XLA Ops:
  0.0 265.7 %chain.1 = bf16[128,2304]{1,0:T(8,128)(2,1)} custom-call(bf16[128,2304]{1,0:T(8,128)(2,1)} %bitcast.9, bf16[1152,2304]{1,0:T(8,128)(2,1)} %bitcast.5, bf16[2304,1152]{1,0:T(8,128)(2,1)} %bitcast.6, bf16[8,16,16,1152]{3,2,1,0:T(8,128)(2,1)} %bitcast.7), custom_call_target="tpu_custom_call" | custom-call | tf_op jit(solution)/shard_map/chain/pallas_call | solution.py:265
  265.7 1.9 copy.6

commit v3 on v2

--- a/solution.py
+++ b/solution.py
@@ -9,7 +9,9 @@
 
 MESH = pl.DeviceIdType.MESH
 BLOCK = 16
+ORDER = ((2, 1), (2, 0), (1, 1), (3, 1), (1, 0), (3, 0), (0, 1))
 AHEAD = 3
+PARTS = ((0, 512), (512, 640))
 F32 = jnp.float32
 BF16 = jnp.bfloat16
 NN = (((1,), (0,)), ((), ()))
@@ -22,7 +24,7 @@
 def kernel(
     sections, chips, chunks,
     top_hbm, down_hbm, up_hbm, gate_hbm, out_hbm,
-    top, down_raw, up_raw, down, up, gate, feed, held, act, hidden, grad_up, own_part, sib_part, sib_recv, pair, terms, result, out,
+    down_raw, up_raw, down, up, gate, feed, held, act, hidden, grad_up, own_part, sib_part, sib_recv, pair, terms, result, out,
     load_sem, feed_send, feed_recv, own_sem, hop_send, hop_recv, in_send, in_recv, swap_send, swap_recv, part_send, part_recv,
     term_send, term_recv, out_send, out_recv, store_sem,
 ):
@@ -45,6 +47,11 @@
             device_id={"section": to_section, "tensor": to_tensor}, device_id_type=MESH,
         )
 
+    def peer(step, flip):
+        return lax.rem(lax.div(chip, 2) + step, chips // 2) * 2 + lax.rem(chip + flip, 2)
+
+    parts = [pl.ds(0, half)] if half < 1152 else [pl.ds(start, size) for start, size in PARTS]
+
     def rows_of(index):
         return pl.ds(pl.multiple_of(index * BLOCK, BLOCK), BLOCK)
 
@@ -52,10 +59,9 @@
         return pl.ds(pl.multiple_of(index * half, 128), half)
 
     loads = [
-        pltpu.make_async_copy(top_hbm, top, load_sem.at[0]),
-        pltpu.make_async_copy(gate_hbm, gate, load_sem.at[1]),
-        pltpu.make_async_copy(down_hbm, down_raw, load_sem.at[2]),
-        pltpu.make_async_copy(up_hbm, up_raw, load_sem.at[3]),
+        pltpu.make_async_copy(gate_hbm, gate, load_sem.at[0]),
+        pltpu.make_async_copy(down_hbm, down_raw, load_sem.at[1]),
+        pltpu.make_async_copy(up_hbm, up_raw, load_sem.at[2]),
     ]
     for load in loads:
         load.start()
@@ -83,54 +89,55 @@
 
     pl.semaphore_wait(barrier, chips + jnp.where(section > 0, 1, 0) + jnp.where(section < last, 1, 0))
 
-    loads[0].wait()
-
-    def spread(block, c, index):
-        for step in range(1, chips):
+    def spread(block, c, index, p):
+        for relation in ORDER:
             remote(
-                block, held.at[c, core, rows_of(index)], in_send.at[c], in_recv.at[c],
-                section, lax.rem(chip + step, chips) * 2 + core,
+                block, held.at[c, core, rows_of(index), parts[p]], in_send.at[c, p], in_recv.at[c, p],
+                section, peer(*relation) * 2 + core,
             ).start()
 
     def send_feed(c):
-        block = feed.at[pl.ds(pl.multiple_of(c * BLOCK, BLOCK), BLOCK)]
-        spread(block, c, chip)
-        pltpu.make_async_copy(block, held.at[c, core, rows_of(chip)], hop_recv.at[c]).start()
+        for p, cols in enumerate(parts):
+            block = feed.at[rows_of(c), cols]
+            spread(block, c, chip, p)
+            pltpu.make_async_copy(block, held.at[c, core, rows_of(chip), cols], hop_recv.at[c, p]).start()
 
     def forward(c):
-        block = held.at[c, core, rows_of(facing)]
-        wait_for(block, hop_recv.at[c])
-        spread(block, c, facing)
+        for p, cols in enumerate(parts):
+            block = held.at[c, core, rows_of(facing), cols]
+            wait_for(block, hop_recv.at[c, p])
+            spread(block, c, facing, p)
 
     rows_here = per_core * BLOCK
 
     @pl.when(section == last)
     def _():
         mine = feed.at[pl.ds(pl.multiple_of(core * rows_here, BLOCK), rows_here)]
-        swap = remote(top.at[:, cols_of(other)], mine, feed_send, feed_recv, section, sibling)
+        swap = remote(top_hbm.at[:, cols_of(other)], mine, feed_send, feed_recv, section, sibling)
         swap.start()
-        keep = pltpu.make_async_copy(top.at[:, cols_of(core)], mine, own_sem)
+        keep = pltpu.make_async_copy(top_hbm.at[:, cols_of(core)], mine, own_sem)
         keep.start()
         keep.wait()
         swap.wait()
         for c in range(min(AHEAD, chunks)):
             send_feed(c)
 
-    loads[1].wait()
+    loads[0].wait()
 
     def finish(c):
-        wait_for(terms.at[c, pl.ds(0, chips - 1)], term_recv.at[c])
-        total = held[c, core, rows_of(chip), :].astype(F32)
-        for j in range(chips):
-            total = total + terms[c, j].astype(F32)
-        result[c] = total.astype(BF16)
-
-        @pl.when(section > 0)
-        def _():
-            remote(
-                result.at[c], held.at[c, core, rows_of(chip)], hop_send.at[c], hop_recv.at[c],
-                section - 1, facing * 2 + core,
-            ).start()
+        for p, cols in enumerate(parts):
+            wait_for(terms.at[c, pl.ds(0, chips - 1), :, cols], term_recv.at[c, p])
+            total = held[c, core, rows_of(chip), cols].astype(F32)
+            for j in range(chips):
+                total = total + terms[c, j, :, cols].astype(F32)
+            result[c, :, cols] = total.astype(BF16)
+
+            @pl.when(section > 0)
+            def _():
+                remote(
+                    result.at[c, :, cols], held.at[c, core, rows_of(chip), cols],
+                    hop_send.at[c, p], hop_recv.at[c, p], section - 1, facing * 2 + core,
+                ).start()
 
         place = lax.rem(c, per_core)
 
@@ -147,52 +154,61 @@
     def chunk_step(c, carry):
         act[...] = gelu(gate[:, c].reshape(chips * BLOCK, -1).astype(F32))
 
-        @pl.when(section == last)
-        def _():
-            wait_for(held.at[c, core, rows_of(chip)], hop_recv.at[c])
-
-        wait_for(terms.at[c, pl.ds(0, chips - 1)], in_recv.at[c])
-        remote(
-            held.at[c, core], held.at[c, core], swap_send.at[c], swap_recv.at[c], section, sibling
-        ).start()
-
-        hidden[...] = lax.dot_general(held[c, core], down[core], NN, preferred_element_type=F32)
+        for p, cols in enumerate(parts):
+            @pl.when(section == last)
+            def _():
+                wait_for(held.at[c, core, rows_of(chip), cols], hop_recv.at[c, p])
+
+            wait_for(terms.at[c, pl.ds(0, chips - 1), :, cols], in_recv.at[c, p])
+            remote(
+                held.at[c, core, :, cols], held.at[c, core, :, cols], swap_send.at[c, p], swap_recv.at[c, p],
+                section, sibling,
+            ).start()
+            term = lax.dot_general(
+                held[c, core, :, cols], down[core, cols, :], NN, preferred_element_type=F32
+            )
+            hidden[...] = term if p == 0 else hidden[...] + term
 
         @pl.when((section < last) & (c + 1 < chunks))
         def _():
             forward(c + 1)
 
-        wait_for(held.at[c, other], swap_recv.at[c])
-        total = hidden[...] + lax.dot_general(
-            held[c, other], down[other], NN, preferred_element_type=F32
-        )
+        total = hidden[...]
+        for p, cols in enumerate(parts):
+            wait_for(held.at[c, other, :, cols], swap_recv.at[c, p])
+            total = total + lax.dot_general(
+                held[c, other, :, cols], down[other, cols, :], NN, preferred_element_type=F32
+            )
         grad_up[...] = (total * act[...]).astype(BF16)
 
-        sib_part[c] = lax.dot_general(
-            grad_up[...], up[other], NN, preferred_element_type=F32
-        ).astype(BF16)
-        remote(
-            sib_part.at[c], sib_recv.at[c], part_send.at[c], part_recv.at[c], section, sibling
-        ).start()
+        for p, cols in enumerate(parts):
+            sib_part[c, :, cols] = lax.dot_general(
+                grad_up[...], up[other, :, cols], NN, preferred_element_type=F32
+            ).astype(BF16)
+            remote(
+                sib_part.at[c, :, cols], sib_recv.at[c, :, cols], part_send.at[c, p], part_recv.at[c, p],
+                section, sibling,
+            ).start()
         own_part[...] = lax.dot_general(grad_up[...], up[core], NN, preferred_element_type=F32)
 
-        wait_for(sib_recv.at[c], part_recv.at[c])
-        pair[c] = (own_part[...] + sib_recv[c].astype(F32)).astype(BF16)
-        for step in range(1, chips):
-            to_chip = lax.rem(chip + step, chips)
-            remote(
-                pair.at[c, rows_of(to_chip)], terms.at[c, chip], term_send.at[c], term_recv.at[c],
-                section, to_chip * 2 + core,
-            ).start()
+        @pl.when(c > 0)
+        def _():
+            finish(c - 1)
+
+        for p, cols in enumerate(parts):
+            wait_for(sib_recv.at[c, :, cols], part_recv.at[c, p])
+            pair[c, :, cols] = (own_part[:, cols] + sib_recv[c, :, cols].astype(F32)).astype(BF16)
+            for relation in ORDER:
+                to_chip = peer(*relation)
+                remote(
+                    pair.at[c, rows_of(to_chip), cols], terms.at[c, chip, :, cols],
+                    term_send.at[c, p], term_recv.at[c, p], section, to_chip * 2 + core,
+                ).start()
         terms[c, chip] = pair[c, rows_of(chip), :]
 
         @pl.when((section == last) & (c + AHEAD < chunks))
         def _():
             send_feed(c + AHEAD)
-
-        @pl.when(c > 0)
-        def _():
-            finish(c - 1)
 
         return carry
 
@@ -212,9 +228,9 @@
             ].T
         return carry
 
+    loads[1].wait()
+    lax.fori_loop(0, tiles, turn_down, 0)
     loads[2].wait()
-    lax.fori_loop(0, tiles, turn_down, 0)
-    loads[3].wait()
     lax.fori_loop(0, tiles, turn_up, 0)
 
     @pl.when(section < last)
@@ -233,15 +249,16 @@
         store.start()
 
     def drain(c, carry):
-        wait_for(held.at[c, core], swap_send.at[c])
-        wait_for(sib_part.at[c], part_send.at[c])
-        wait_for(terms.at[c, pl.ds(0, chips - 1)], term_send.at[c])
-
-        wait_for(terms.at[c, pl.ds(0, chips - 1)], in_send.at[c])
-
-        @pl.when(section > 0)
-        def _():
-            wait_for(result.at[c], hop_send.at[c])
+        for p, cols in enumerate(parts):
+            seven = terms.at[c, pl.ds(0, chips - 1), :, cols]
+            wait_for(held.at[c, core, :, cols], swap_send.at[c, p])
+            wait_for(sib_part.at[c, :, cols], part_send.at[c, p])
+            wait_for(seven, term_send.at[c, p])
+            wait_for(seven, in_send.at[c, p])
+
+            @pl.when(section > 0)
+            def _():
+                wait_for(result.at[c, :, cols], hop_send.at[c, p])
 
         return carry
 
@@ -269,7 +286,6 @@
         in_specs=[pl.BlockSpec(memory_space=pl.ANY)] * 4,
         out_specs=pl.BlockSpec(memory_space=pl.ANY),
         scratch_shapes=[
-            pltpu.VMEM((row_count, features), BF16),
             pltpu.VMEM((units, features), BF16),
             pltpu.VMEM((features, units), BF16),
             pltpu.VMEM((2, half, units), BF16),
@@ -287,20 +303,20 @@
             pltpu.VMEM((chunks, chips, BLOCK, half), BF16),
             pltpu.VMEM((chunks, BLOCK, half), BF16),
             pltpu.VMEM((2, row_count, half), BF16),
-            dma((4,)),
-            dma,
-            dma,
-            dma,
-            dma((chunks,)),
-            dma((chunks,)),
-            dma((chunks,)),
-            dma((chunks,)),
-            dma((chunks,)),
-            dma((chunks,)),
-            dma((chunks,)),
-            dma((chunks,)),
-            dma((chunks,)),
-            dma((chunks,)),
+            dma((3,)),
+            dma,
+            dma,
+            dma,
+            dma((chunks, 2)),
+            dma((chunks, 2)),
+            dma((chunks, 2)),
+            dma((chunks, 2)),
+            dma((chunks, 2)),
+            dma((chunks, 2)),
+            dma((chunks, 2)),
+            dma((chunks, 2)),
+            dma((chunks, 2)),
+            dma((chunks, 2)),
             dma,
             dma,
             dma((2,)),

time: 268 us -> 259 us (0.966)
  Pallas kernels: 266 us -> 257 us
    pallas_call x1, Pallas kernels: 266 us -> 257 us  [on_device(): pl.pallas_call(functools.partial(kernel, sections, chips, chunks), name='...]
where the time goes in v3:
time: 259 us
  Pallas kernels  257 us (99%)
    pallas_call x1, Pallas kernels, on_device(): pl.pallas_call(functools.partial(kernel, sections, chips, chunks), name='...  257 us

profile of v3, /device:TPU:1, one launch (start us, length us, event | category | flops | bytes accessed | tf_op | source)
XLA Modules:
  0.0 258.6 jit_solution(10246733931238367622)
XLA Ops:
  0.0 256.7 %chain.1 = bf16[128,2304]{1,0:T(8,128)(2,1)} custom-call(bf16[128,2304]{1,0:T(8,128)(2,1)} %bitcast.9, bf16[1152,2304]{1,0:T(8,128)(2,1)} %bitcast.5, bf16[2304,1152]{1,0:T(8,128)(2,1)} %bitcast.6, bf16[8,16,16,1152]{3,2,1,0:T(8,128)(2,1)} %bitcast.7), custom_call_target="tpu_custom_call" | custom-call | tf_op jit(solution)/shard_map/chain/pallas_call | solution.py:282
  256.7 1.9 copy.6

commit v4 on v3

--- a/solution.py
+++ b/solution.py
@@ -9,9 +9,8 @@
 
 MESH = pl.DeviceIdType.MESH
 BLOCK = 16
-ORDER = ((2, 1), (2, 0), (1, 1), (3, 1), (1, 0), (3, 0), (0, 1))
+ORDER = ((2, 1), (1, 1), (3, 1), (2, 0), (1, 0), (3, 0), (0, 1))
 AHEAD = 3
-PARTS = ((0, 512), (512, 640))
 F32 = jnp.float32
 BF16 = jnp.bfloat16
 NN = (((1,), (0,)), ((), ()))
@@ -24,9 +23,9 @@
 def kernel(
     sections, chips, chunks,
     top_hbm, down_hbm, up_hbm, gate_hbm, out_hbm,
-    down_raw, up_raw, down, up, gate, feed, held, act, hidden, grad_up, own_part, sib_part, sib_recv, pair, terms, result, out,
+    down_raw, up_raw, down, up, gate, feed, held, act, hidden, grad_up, own_part, sib_part, sib_recv, pair, terms, result,
     load_sem, feed_send, feed_recv, own_sem, hop_send, hop_recv, in_send, in_recv, swap_send, swap_recv, part_send, part_recv,
-    term_send, term_recv, out_send, out_recv, store_sem,
+    term_send, term_recv, out_send, out_recv, out_own,
 ):
     section = lax.axis_index("section")
     tensor = lax.axis_index("tensor")
@@ -50,7 +49,8 @@
     def peer(step, flip):
         return lax.rem(lax.div(chip, 2) + step, chips // 2) * 2 + lax.rem(chip + flip, 2)
 
-    parts = [pl.ds(0, half)] if half < 1152 else [pl.ds(start, size) for start, size in PARTS]
+    first = half // 256 * 128
+    parts = [pl.ds(0, first), pl.ds(first, half - first)]
 
     def rows_of(index):
         return pl.ds(pl.multiple_of(index * BLOCK, BLOCK), BLOCK)
@@ -92,7 +92,7 @@
     def spread(block, c, index, p):
         for relation in ORDER:
             remote(
-                block, held.at[c, core, rows_of(index), parts[p]], in_send.at[c, p], in_recv.at[c, p],
+                block, held.at[c, core, rows_of(index), parts[p]], in_send, in_recv.at[c, p],
                 section, peer(*relation) * 2 + core,
             ).start()
 
@@ -124,31 +124,32 @@
 
     loads[0].wait()
 
-    def finish(c):
-        for p, cols in enumerate(parts):
-            wait_for(terms.at[c, pl.ds(0, chips - 1), :, cols], term_recv.at[c, p])
-            total = held[c, core, rows_of(chip), cols].astype(F32)
-            for j in range(chips):
-                total = total + terms[c, j, :, cols].astype(F32)
-            result[c, :, cols] = total.astype(BF16)
-
-            @pl.when(section > 0)
-            def _():
-                remote(
-                    result.at[c, :, cols], held.at[c, core, rows_of(chip), cols],
-                    hop_send.at[c, p], hop_recv.at[c, p], section - 1, facing * 2 + core,
-                ).start()
-
-        place = lax.rem(c, per_core)
+    def finish_part(c, p):
+        cols = parts[p]
+        wait_for(terms.at[c, pl.ds(0, chips - 1), :, cols], term_recv.at[c, p])
+        total = held[c, core, rows_of(chip), cols].astype(F32)
+        for j in range(chips):
+            total = total + terms[c, j, :, cols].astype(F32)
+        result[c, :, cols] = total.astype(BF16)
+
+        @pl.when(section > 0)
+        def _():
+            remote(
+                result.at[c, :, cols], held.at[c, core, rows_of(chip), cols],
+                hop_send, hop_recv.at[c, p], section - 1, facing * 2 + core,
+            ).start()
+
+    def place_result(c):
+        rows = rows_of(lax.rem(c, per_core))
 
         @pl.when(lax.div(c, per_core) == core)
         def _():
-            out[core, rows_of(place), :] = result[c]
+            pltpu.make_async_copy(result.at[c], out_hbm.at[rows, cols_of(core)], out_own).start()
 
         @pl.when(lax.div(c, per_core) == other)
         def _():
             remote(
-                result.at[c], out.at[core, rows_of(place)], out_send, out_recv, section, sibling
+                result.at[c], out_hbm.at[rows, cols_of(core)], out_send, out_recv, section, sibling
             ).start()
 
     def chunk_step(c, carry):
@@ -161,7 +162,7 @@
 
             wait_for(terms.at[c, pl.ds(0, chips - 1), :, cols], in_recv.at[c, p])
             remote(
-                held.at[c, core, :, cols], held.at[c, core, :, cols], swap_send.at[c, p], swap_recv.at[c, p],
+                held.at[c, core, :, cols], held.at[c, core, :, cols], swap_send, swap_recv.at[c, p],
                 section, sibling,
             ).start()
             term = lax.dot_general(
@@ -186,14 +187,15 @@
                 grad_up[...], up[other, :, cols], NN, preferred_element_type=F32
             ).astype(BF16)
             remote(
-                sib_part.at[c, :, cols], sib_recv.at[c, :, cols], part_send.at[c, p], part_recv.at[c, p],
+                sib_part.at[c, :, cols], sib_recv.at[c, :, cols], part_send, part_recv.at[c, p],
                 section, sibling,
             ).start()
+
+        @pl.when(c > 0)
+        def _():
+            finish_part(c - 1, 0)
+
         own_part[...] = lax.dot_general(grad_up[...], up[core], NN, preferred_element_type=F32)
-
-        @pl.when(c > 0)
-        def _():
-            finish(c - 1)
 
         for p, cols in enumerate(parts):
             wait_for(sib_recv.at[c, :, cols], part_recv.at[c, p])
@@ -202,8 +204,15 @@
                 to_chip = peer(*relation)
                 remote(
                     pair.at[c, rows_of(to_chip), cols], terms.at[c, chip, :, cols],
-                    term_send.at[c, p], term_recv.at[c, p], section, to_chip * 2 + core,
+                    term_send, term_recv.at[c, p], section, to_chip * 2 + core,
                 ).start()
+
+            if p == 0:
+                @pl.when(c > 0)
+                def _():
+                    finish_part(c - 1, 1)
+                    place_result(c - 1)
+
         terms[c, chip] = pair[c, rows_of(chip), :]
 
         @pl.when((section == last) & (c + AHEAD < chunks))
@@ -238,34 +247,22 @@
         forward(0)
 
     lax.fori_loop(0, chunks, chunk_step, 0)
-    finish(chunks - 1)
-
-    wait_for(out.at[other], out_recv)
-    stores = [
-        pltpu.make_async_copy(out.at[h], out_hbm.at[:, pl.ds(h * half, half)], store_sem.at[h])
-        for h in range(2)
-    ]
-    for store in stores:
-        store.start()
-
-    def drain(c, carry):
-        for p, cols in enumerate(parts):
-            seven = terms.at[c, pl.ds(0, chips - 1), :, cols]
-            wait_for(held.at[c, core, :, cols], swap_send.at[c, p])
-            wait_for(sib_part.at[c, :, cols], part_send.at[c, p])
-            wait_for(seven, term_send.at[c, p])
-            wait_for(seven, in_send.at[c, p])
-
-            @pl.when(section > 0)
-            def _():
-                wait_for(result.at[c, :, cols], hop_send.at[c, p])
-
-        return carry
-
-    lax.fori_loop(0, chunks, drain, 0)
-    wait_for(out.at[core], out_send)
-    for store in stores:
-        store.wait()
+    for p in range(len(parts)):
+        finish_part(chunks - 1, p)
+    place_result(chunks - 1)
+
+    wait_for(feed.at[pl.ds(0, rows_here)], out_own)
+    wait_for(feed.at[pl.ds(0, rows_here)], out_recv)
+    wait_for(held.at[:, core], swap_send)
+    wait_for(sib_part, part_send)
+    wait_for(terms.at[:, pl.ds(0, chips - 1)], term_send)
+    wait_for(terms.at[:, pl.ds(0, chips - 1)], in_send)
+
+    @pl.when(section > 0)
+    def _():
+        wait_for(result, hop_send)
+
+    wait_for(feed.at[pl.ds(0, rows_here)], out_send)
 
 
 def on_device(sections, top_grad, down_weight, up_weight, gate_pre):
@@ -302,24 +299,23 @@
             pltpu.VMEM((chunks, rows, half), BF16),
             pltpu.VMEM((chunks, chips, BLOCK, half), BF16),
             pltpu.VMEM((chunks, BLOCK, half), BF16),
-            pltpu.VMEM((2, row_count, half), BF16),
             dma((3,)),
             dma,
             dma,
             dma,
-            dma((chunks, 2)),
-            dma((chunks, 2)),
-            dma((chunks, 2)),
-            dma((chunks, 2)),
-            dma((chunks, 2)),
-            dma((chunks, 2)),
-            dma((chunks, 2)),
-            dma((chunks, 2)),
-            dma((chunks, 2)),
-            dma((chunks, 2)),
-            dma,
-            dma,
-            dma((2,)),
+            dma,
+            dma((chunks, 2)),
+            dma,
+            dma((chunks, 2)),
+            dma,
+            dma((chunks, 2)),
+            dma,
+            dma((chunks, 2)),
+            dma,
+            dma((chunks, 2)),
+            dma,
+            dma,
+            dma,
         ],
         compiler_params=pltpu.CompilerParams(
             collective_id=0, has_side_effects=True, vmem_limit_bytes=60 * 1024 * 1024

time: 259 us -> 255 us (0.985)
  Pallas kernels: 257 us -> 253 us
    pallas_call x1, Pallas kernels: 257 us -> 253 us  [on_device(): pl.pallas_call(functools.partial(kernel, sections, chips, chunks), name='...]
where the time goes in v4:
time: 255 us
  Pallas kernels  253 us (99%)
    pallas_call x1, Pallas kernels, on_device(): pl.pallas_call(functools.partial(kernel, sections, chips, chunks), name='...  253 us

profile of v4, /device:TPU:1, one launch (start us, length us, event | category | flops | bytes accessed | tf_op | source)
XLA Modules:
  0.0 255.0 jit_solution(8873170360879816750)
XLA Ops:
  0.0 253.1 %chain.1 = bf16[128,2304]{1,0:T(8,128)(2,1)} custom-call(bf16[128,2304]{1,0:T(8,128)(2,1)} %bitcast.9, bf16[1152,2304]{1,0:T(8,128)(2,1)} %bitcast.5, bf16[2304,1152]{1,0:T(8,128)(2,1)} %bitcast.6, bf16[8,16,16,1152]{3,2,1,0:T(8,128)(2,1)} %bitcast.7), custom_call_target="tpu_custom_call" | custom-call | tf_op jit(solution)/shard_map/chain/pallas_call | solution.py:279
  253.1 1.9 copy.6

commit v5 on v4

--- a/solution.py
+++ b/solution.py
@@ -9,7 +9,7 @@
 
 MESH = pl.DeviceIdType.MESH
 BLOCK = 16
-ORDER = ((2, 1), (1, 1), (3, 1), (2, 0), (1, 0), (3, 0), (0, 1))
+ORDER = ((2, 1), (1, 1), (3, 1), (0, 1), (2, 0), (1, 0), (3, 0))
 AHEAD = 3
 F32 = jnp.float32
 BF16 = jnp.bfloat16
@@ -112,15 +112,26 @@
 
     @pl.when(section == last)
     def _():
-        mine = feed.at[pl.ds(pl.multiple_of(core * rows_here, BLOCK), rows_here)]
-        swap = remote(top_hbm.at[:, cols_of(other)], mine, feed_send, feed_recv, section, sibling)
-        swap.start()
-        keep = pltpu.make_async_copy(top_hbm.at[:, cols_of(core)], mine, own_sem)
-        keep.start()
-        keep.wait()
-        swap.wait()
+        ready = min(AHEAD, per_core)
+        pieces = [(0, ready * BLOCK), (ready * BLOCK, rows_here - ready * BLOCK)]
+        moves = []
+        for q, (start, size) in enumerate(pieces):
+            if size:
+                mine = feed.at[pl.ds(pl.multiple_of(core * rows_here + start, BLOCK), size)]
+                theirs = top_hbm.at[pl.ds(start, size), cols_of(other)]
+                swap = remote(theirs, mine, feed_send.at[q], feed_recv.at[q], section, sibling)
+                keep = pltpu.make_async_copy(top_hbm.at[pl.ds(start, size), cols_of(core)], mine, own_sem.at[q])
+                swap.start()
+                keep.start()
+                moves.append((swap, keep))
         for c in range(min(AHEAD, chunks)):
+            if c % ready == 0 and c // ready < len(moves):
+                for move in moves[c // ready]:
+                    move.wait()
             send_feed(c)
+        for swap, keep in moves[(min(AHEAD, chunks) - 1) // ready + 1:]:
+            swap.wait()
+            keep.wait()
 
     loads[0].wait()
 
@@ -300,9 +311,9 @@
             pltpu.VMEM((chunks, chips, BLOCK, half), BF16),
             pltpu.VMEM((chunks, BLOCK, half), BF16),
             dma((3,)),
-            dma,
-            dma,
-            dma,
+            dma((2,)),
+            dma((2,)),
+            dma((2,)),
             dma,
             dma((chunks, 2)),
             dma,

time: 255 us -> 255 us (level)
  no operation moved by 1% of the time
where the time goes in v5:
time: 255 us
  Pallas kernels  253 us (99%)
    pallas_call x1, Pallas kernels, on_device(): pl.pallas_call(functools.partial(kernel, sections, chips, chunks), name='...  253 us

profile of v5, /device:TPU:1, one launch (start us, length us, event | category | flops | bytes accessed | tf_op | source)
XLA Modules:
  0.0 254.9 jit_solution(6801123431322066512)
XLA Ops:
  0.0 252.9 %chain.1 = bf16[128,2304]{1,0:T(8,128)(2,1)} custom-call(bf16[128,2304]{1,0:T(8,128)(2,1)} %bitcast.9, bf16[1152,2304]{1,0:T(8,128)(2,1)} %bitcast.5, bf16[2304,1152]{1,0:T(8,128)(2,1)} %bitcast.6, bf16[8,16,16,1152]{3,2,1,0:T(8,128)(2,1)} %bitcast.7), custom_call_target="tpu_custom_call" | custom-call | tf_op jit(solution)/shard_map/chain/pallas_call | solution.py:290
  252.9 1.9 copy.6
